TPU v7x, 32 devices: a whole 2x2x4 slice. The times are simulated.
32 devices in a mesh: groups: 2 (over y), expert: 8 (over z, core), dp: 2 (over x), node: 1.
Axes of the slice: x: 2, y: 2, z: 4, core: 2. Of those that a mesh axis runs over, the one named last changes fastest.
Arguments:
- grad_out: bfloat16 [4096, 4096], P(('groups', 'expert', 'dp', 'node')), parts along dimension 0, may hold values from -4 to 4
- routes: int32 [4096, 4], P(('groups', 'expert', 'dp', 'node')), parts along dimension 0, may hold values from 0 to 7, all different within a row; in each aligned block of 128 rows (0 to 127, 128 to 255, ...) at most 68 rows name the same one
- gates: bfloat16 [4096, 4], P(('groups', 'expert', 'dp', 'node')), parts along dimension 0, may hold values from 0.049804688 to 1
- gate_pre: bfloat16 [16, 2, 8, 68, 768], P(('groups', 'expert'), 'dp', None, None, 'node'), parts along dimension 0, may hold values from -6 to 6
- up_pre: bfloat16 [16, 2, 8, 68, 768], P(('groups', 'expert'), 'dp', None, None, 'node'), parts along dimension 0, may hold values from -6 to 6
- w_down: bfloat16 [8, 4096, 768], P('expert', 'dp', 'node'), may hold values from -0.21875 to 0.21875
Outputs:
- d_gates: float32 [4096, 4], P(('groups', 'expert', 'dp', 'node')), parts along dimension 0
- d_gate_pre: bfloat16 [16, 2, 8, 68, 768], P(('groups', 'expert'), 'dp', None, None, 'node'), parts along dimension 0
- d_up_pre: bfloat16 [16, 2, 8, 68, 768], P(('groups', 'expert'), 'dp', None, None, 'node'), parts along dimension 0
- d_w_down: bfloat16 [16, 4096, 768], P(('groups', 'expert'), 'dp', 'node'), parts along dimension 0
There are 2 independent parts, one for each index of `groups`. A program takes and returns all parts, laid end to end along the dimension named above; an argument that names none is the same for every part. Nothing has to cross between parts.
Inputs may be any that keep to these rules, and one draw needn't show every extreme that they name: `routes`: in the rows of one device no expert is named by more than 68 entries, a bound that some block reaches of them; the 4 experts of a token differ.
All inputs are finite; a program needn't handle non-finite values.
Results may differ from a plain program's by a relative error of at most 0.017.
Values may be sent and summed in bfloat16 or wider, within the bound.
A program may use at most 128 MiB of HBM per device.

v0:
```python
import jax
import jax.numpy as jnp
from jax import lax
from jax.sharding import PartitionSpec as P


def local(grad_out, routes, gates, gate_pre, up_pre, w_down):
    tok_rows, width = grad_out.shape
    topk = routes.shape[1]
    sources = gate_pre.shape[2]
    capacity = gate_pre.shape[3]
    hidden = gate_pre.shape[4]
    experts = lax.axis_size("expert")
    node_count = lax.axis_size("node")
    count = tok_rows * topk
    slot_count = sources * capacity
    flat_routes = routes.reshape(count)
    member = (flat_routes[:, None] == jnp.arange(experts, dtype=jnp.int32)[None, :]).astype(
        jnp.int32
    )
    rank = jnp.sum(jnp.cumsum(member, axis=0) * member, axis=1) - 1
    slot_of = flat_routes * capacity + rank
    placer = jnp.arange(experts * capacity, dtype=jnp.int32)[:, None] == slot_of[None, :]
    placer_f = placer.astype(jnp.float32)
    by_token = jnp.sum(
        placer.reshape(experts * capacity, tok_rows, topk).astype(jnp.int32), axis=2
    ).astype(jnp.bfloat16)
    send_rows = (
        jnp.dot(by_token, grad_out, preferred_element_type=jnp.float32)
        .astype(jnp.bfloat16)
        .reshape(experts, capacity, width)
    )
    send_gates = (
        jnp.dot(placer_f, gates.reshape(count).astype(jnp.float32), precision=lax.Precision.HIGHEST)
        .astype(jnp.bfloat16)
        .reshape(experts, capacity)
    )
    pair_rows, pair_gates = (
        lax.all_gather(send_rows[None], "node", axis=0, tiled=True),
        lax.all_gather(send_gates[None], "node", axis=0, tiled=True),
    )
    recv_rows, recv_gates = (
        lax.all_to_all(pair_rows, "expert", split_axis=1, concat_axis=0, tiled=True),
        lax.all_to_all(pair_gates, "expert", split_axis=1, concat_axis=0, tiled=True),
    )
    rows = recv_rows.reshape(slot_count, width)
    gate_col = recv_gates.reshape(slot_count).astype(jnp.float32)
    pre_a = gate_pre.reshape(slot_count, hidden).astype(jnp.float32)
    pre_u = up_pre.reshape(slot_count, hidden).astype(jnp.float32)
    columns = rows
    grad_h = jnp.dot(
        columns,
        lax.all_gather(w_down, "dp", axis=1, tiled=True)[0],
        preferred_element_type=jnp.float32,
    )
    sig = jax.nn.sigmoid(pre_a)
    act = pre_a * sig
    hact = act * pre_u
    partial_score = jnp.sum(grad_h * hact, axis=1)
    d_act = gate_col[:, None] * grad_h
    d_a = (
        (d_act * pre_u * sig * (1.0 + pre_a * (1.0 - sig)))
        .astype(jnp.bfloat16)
        .reshape(gate_pre.shape)
    )
    d_u = (d_act * act).astype(jnp.bfloat16).reshape(up_pre.shape)
    weighted = (gate_col[:, None] * hact).astype(jnp.bfloat16)
    columns = rows
    grad_w = lax.psum_scatter(
        lax.dot_general(
            columns, weighted, (((0,), (0,)), ((), ())), preferred_element_type=jnp.float32
        ).astype(jnp.bfloat16),
        "dp",
        scatter_dimension=0,
        tiled=True,
    )
    d_w = grad_w[None]
    returned = lax.all_to_all(
        partial_score.reshape(sources, 1, capacity),
        ("expert", "node"),
        split_axis=0,
        concat_axis=1,
        tiled=True,
    )
    summed = jnp.sum(returned.reshape(experts, node_count, capacity), axis=1).reshape(
        experts * capacity
    )
    d_gates = jnp.dot(summed, placer_f, precision=lax.Precision.HIGHEST).reshape(tok_rows, topk)
    return (d_gates, d_a, d_u, d_w)


def solution(mesh):
    placed = (
        P(("groups", "expert", "dp", "node"), None),
        P(("groups", "expert", "dp", "node"), None),
        P(("groups", "expert", "dp", "node"), None),
        P(("groups", "expert"), "dp", None, None, "node"),
        P(("groups", "expert"), "dp", None, None, "node"),
        P("expert", "dp", "node"),
    )
    return jax.shard_map(
        local,
        mesh=mesh,
        in_specs=placed,
        out_specs=(
            P(("groups", "expert", "dp", "node"), None),
            P(("groups", "expert"), "dp", None, None, "node"),
            P(("groups", "expert"), "dp", None, None, "node"),
            P(("groups", "expert"), "dp", "node"),
        ),
        check_vma=False,
    )
```

profile of v0, /device:TPU:0, one launch (start us, length us, event | category | flops | bytes accessed | tf_op | source)
XLA Modules:
  0.0 235.6 jit_solution(1975691823631817453)
XLA Ops:
  7.2 0.0 copy-start
  7.2 0.9 copy.53
  8.1 0.1 eq.65
  8.2 0.1 eq.61
  8.3 1.1 reduce-window.6
  9.4 0.2 slice_reduce_fusion
  9.7 0.1 fusion.7
  9.8 0.8 copy.59
  10.6 0.1 reshape.145
  10.7 0.3 fusion.4
  11.0 0.7 broadcast_in_dim_reshape.9
  11.7 6.3 %all-to-all-start.2 = ((bf16[1,8,68]{2,0,1:T(2,128)(2,1)}), bf16[1,8,68]{2,0,1:T(2,128)(2,1)S(1)}, u32[]{:S(2)}, u32[]{:S(2)}) async-start(bf16[1,8,68]{2,0,1:T(2,128)(2,1)} %broadcast_in_dim_reshape.9), calls=%async_computation.2 | async-start | bytes 8192 | tf_op jit(solution)/shard_map/all_to_all | solution.py:44
  18.1 0.1 sub.10
  18.2 0.1 copy.55
  18.2 0.7 multiply_add_fusion.1
  18.9 0.1 convert_reduce_fusion
  19.1 0.0 copy-done
  19.1 3.4 %convolution_convert_fusion.1 = bf16[544,4096]{1,0:T(8,128)(2,1)} fusion(bf16[128,4096]{1,0:T(8,128)(2,1)S(1)} %copy-done, s32[544,128]{1,0:T(8,128)S(1)} %convert_reduce_fusion), kind=kOutput, calls=%fused_computation.3 | convolution fusion | flops 572723200 | bytes 5783552 | tf_op jit(solution)/shard_map/dot_general | solution.py:29
  22.4 5.2 %broadcast_in_dim_reshape.7 = bf16[1,8,68,4096]{3,2,1,0:T(8,128)(2,1)} reshape(bf16[544,4096]{1,0:T(8,128)(2,1)} %convolution_convert_fusion.1) | data formatting | bytes 8912896 | tf_op jit(solution)/shard_map/broadcast_in_dim;reshape | solution.py:39
  27.6 0.0 all-to-all-done.2
  27.7 5.1 %all-to-all-start = ((bf16[1,8,68,4096]{3,2,0,1:T(8,128)(2,1)}), bf16[1,8,68,4096]{3,2,0,1:T(8,128)(2,1)}, u32[]{:S(2)}, u32[]{:S(2)}) async-start(bf16[1,8,68,4096]{3,2,0,1:T(8,128)(2,1)} %bitcast.23), calls=%async_computation | async-start | bytes 9437184 | tf_op jit(solution)/shard_map/all_to_all | solution.py:43
  32.7 0.0 copy-start.1
  32.8 0.0 copy-start.2
  32.8 0.0 all-gather.2.cloned.1.call-start
  32.8 0.7 all-gather.2.cloned.1.call-update
  33.5 0.0 reduce-scatter.2.cloned.1.call-start
  33.6 0.1 copy.61
  33.7 0.2 copy-done.1
  33.9 0.3 copy-done.2
  34.2 0.6 multiply_convert_fusion
  34.7 0.1 copy.62
  34.9 1.0 convert_element_type.86
  35.9 0.0 copy-start.4
  35.9 102.2 %all-to-all-done = bf16[1,8,68,4096]{3,2,0,1:T(8,128)(2,1)} async-done(((bf16[1,8,68,4096]{3,2,0,1:T(8,128)(2,1)}), bf16[1,8,68,4096]{3,2,0,1:T(8,128)(2,1)}, u32[]{:S(2)}, u32[]{:S(2)}) %all-to-all-start) | async-done | bytes 4456480 | tf_op jit(solution)/shard_map/all_to_all | solution.py:43
  138.1 5.2 %reshape.133 = bf16[544,4096]{1,0:T(8,128)(2,1)} reshape(bf16[1,8,68,4096]{3,2,0,1:T(8,128)(2,1)} %all-to-all-done) | data formatting | bytes 8912896 | tf_op jit(solution)/shard_map/reshape | solution.py:46
  143.3 0.0 copy-done.4
  143.3 9.3 %convolution_convert_fusion = bf16[4096,768]{1,0:T(8,128)(2,1)} fusion(bf16[544,4096]{1,0:T(8,128)(2,1)} %reshape.133, bf16[544,768]{1,0:T(8,128)(2,1)S(1)} %copy-done.4), kind=kOutput, calls=%fused_computation | convolution fusion | flops 3425697792 | bytes 11583488 | tf_op jit(solution)/shard_map/dot_general | solution.py:70
  152.7 0.0 reduce-scatter.2.cloned.1.call-update
  152.7 0.0 copy-start.3
  152.7 1.4 copy.57
  154.1 0.0 copy-done.3
  154.1 0.2 copy.58
  154.3 2.6 %reshape.139 = f32[544,768]{1,0:T(8,128)} reshape(f32[1,1,8,68,768]{4,3,2,1,0:T(8,128)} %copy.57) | data formatting | bytes 3342336 | tf_op jit(solution)/shard_map/convert_element_type | solution.py:48
  156.9 1.4 reshape.140
  158.3 0.1 reshape.141
  158.4 0.0 all-gather.2.cloned.1.call-done
  158.4 10.2 %multiply_convert_fusion.2 = (bf16[544,768]{1,0:T(8,128)(2,1)}, f32[544]{0:T(1024)S(1)}, bf16[544,768]{1,0:T(8,128)(2,1)S(1)}) fusion(f32[544,768]{1,0:T(8,128)} %reshape.139, f32[544,768]{1,0:T(8,128)} %reshape.140, f32[544]{0:T(1024)S(1)} %reshape.141, bf16[544,4096]{1,0:T(8,128)(2,1)} %reshape.133, bf16[1,4096,768]{2,1,0:T(8,128)(2,1)} %all-gather.2.cloned.1.call-done), kind=kOutput, calls=%fused_computation.6 | convolution fusion | flops 3429654016 | bytes 15765760 | tf_op jit(solution)/shard_map/dot_general | solution.py:51
  168.6 0.7 reshape.134
  169.3 3.4 %all-to-all-start.1 = ((f32[8,1,68]{2,1,0:T(1,128)}), f32[8,1,68]{2,1,0:T(1,128)S(1)}, u32[]{:S(2)}, u32[]{:S(2)}) async-start(f32[8,1,68]{2,1,0:T(1,128)} %reshape.134), calls=%async_computation.1 | async-start | bytes 8192 | tf_op jit(solution)/shard_map/all_to_all | solution.py:78
  172.7 0.2 iota_compare_fusion
  172.9 0.2 eq.74
  173.1 1.3 reshape.137
  174.4 1.0 copy.63
  175.5 0.2 reshape.138
  175.6 1.0 copy.64
  176.7 1.6 all-to-all-done.1
  178.2 0.5 broadcast.85
  178.7 0.7 reduce.13
  179.4 0.1 reshape.135
  179.5 0.5 select_reduce_fusion
  180.0 0.7 copy.69
  180.6 48.2 %reduce-scatter.2.cloned.1.call-done = bf16[2048,768]{1,0:T(8,128)(2,1)} async-done(((bf16[4096,768]{1,0:T(8,128)(2,1)}), bf16[2048,768]{1,0:T(8,128)(2,1)}) %reduce-scatter.2.cloned.1.call-update) | async-done | bytes 3145744 | tf_op jit(solution)/shard_map/reduce_scatter | solution.py:69
  (6 shorter events, 0.1 us)
Async XLA Ops:
  7.2 11.9 %copy-start = (bf16[128,4096]{1,0:T(8,128)(2,1)S(1)}, bf16[128,4096]{1,0:T(8,128)(2,1)}, u32[]{:S(2)}) copy-start(bf16[128,4096]{1,0:T(8,128)(2,1)} %param.6) | copy-start | bytes 3145732
  11.7 15.9 %all-to-all-start.2 = ((bf16[1,8,68]{2,0,1:T(2,128)(2,1)}), bf16[1,8,68]{2,0,1:T(2,128)(2,1)S(1)}, u32[]{:S(2)}, u32[]{:S(2)}) async-start(bf16[1,8,68]{2,0,1:T(2,128)(2,1)} %broadcast_in_dim_reshape.9), calls=%async_computation.2 | async-start | bytes 8192 | tf_op jit(solution)/shard_map/all_to_all | solution.py:44
  27.7 110.4 %all-to-all-start = ((bf16[1,8,68,4096]{3,2,0,1:T(8,128)(2,1)}), bf16[1,8,68,4096]{3,2,0,1:T(8,128)(2,1)}, u32[]{:S(2)}, u32[]{:S(2)}) async-start(bf16[1,8,68,4096]{3,2,0,1:T(8,128)(2,1)} %bitcast.23), calls=%async_computation | async-start | bytes 9437184 | tf_op jit(solution)/shard_map/all_to_all | solution.py:43
  32.7 1.1 copy-start.1
  32.8 1.4 copy-start.2
  32.8 125.6 %all-gather.2.cloned.1.call-start = ((), (), s32[]{:S(2)}) async-start(), calls=%async_computation.4 | async-start | bytes 9437184 | tf_op jit(solution)/shard_map/all_gather | solution.py:53
  33.5 195.3 %reduce-scatter.2.cloned.1.call-start = ((), (), s32[]{:S(2)}) async-start(), calls=%async_computation.5 | async-start | bytes 9437184 | tf_op jit(solution)/shard_map/reduce_scatter | solution.py:69
  35.9 107.4 %copy-start.4 = (bf16[544,768]{1,0:T(8,128)(2,1)S(1)}, bf16[544,768]{1,0:T(8,128)(2,1)}, u32[]{:S(2)}) copy-start(bf16[544,768]{1,0:T(8,128)(2,1)} %convert_element_type.86) | copy-start | bytes 2506756
  152.7 1.4 copy-start.3
  169.3 9.0 %all-to-all-start.1 = ((f32[8,1,68]{2,1,0:T(1,128)}), f32[8,1,68]{2,1,0:T(1,128)S(1)}, u32[]{:S(2)}, u32[]{:S(2)}) async-start(f32[8,1,68]{2,1,0:T(1,128)} %reshape.134), calls=%async_computation.1 | async-start | bytes 8192 | tf_op jit(solution)/shard_map/all_to_all | solution.py:78
Sparse Core Ops, SparseCore 0:
  35.1 81.8 all-gather.1
  152.8 75.9 reduce-scatter.1
where the time goes:
time: 236 us
  waiting for transfers between devices  153 us (65%)
  local copies, waits for them, and re-layouts  26.6 us (11%)
  matrix products  23.2 us (10%)
  starting transfers between devices  14.9 us (6%)
  between operations  14.2 us (6%)
  other arithmetic  4.12 us (2%)
    all_to_all x1, waiting for transfers between devices, local(): lax.all_to_all(pair_rows, 'expert', split_axis=1, concat_axis=0, tiled=True)  102 us
    reduce_scatter x1, waiting for transfers between devices, local(): lax.psum_scatter(lax.dot_general(columns, weighted, (((0,), (0,)), ((), (...  48.2 us
    dot_general x1, matrix products, local(): jnp.dot(columns, lax.all_gather(w_down, 'dp', axis=1, tiled=True)[0], pre...  10.2 us
    dot_general x1, matrix products, local(): lax.dot_general(columns, weighted, (((0,), (0,)), ((), ())), preferred_el...  9.34 us
    all_to_all x1, starting transfers between devices, local(): lax.all_to_all(pair_gates, 'expert', split_axis=1, concat_axis=0, tiled=T...  6.33 us
    another operation x1, local copies, waits for them, and re-layouts, local(): send_rows[None]  5.23 us
    reshape x1, local copies, waits for them, and re-layouts, local(): rows = recv_rows.reshape(slot_count, width)  5.21 us
    all_to_all x1, starting transfers between devices, local(): lax.all_to_all(pair_rows, 'expert', split_axis=1, concat_axis=0, tiled=True)  5.1 us
  transfers between devices with their start and end apart: 5, of which 3 were waited for; matrix products, arithmetic and copies ran while one was open for 21% of the time, Pallas kernels for 0%

commit v1 on v0

--- a/solution.py
+++ b/solution.py
@@ -1,7 +1,309 @@
 import jax
 import jax.numpy as jnp
 from jax import lax
+from jax.experimental import pallas as pl
+from jax.experimental.pallas import tpu as pltpu
 from jax.sharding import PartitionSpec as P
+
+
+PAD = 80
+TILE = 512
+
+
+def whole_kernel(
+    meta_ref, gout, gpre, upre, wdn, dg_ref, da_ref, du_ref, dw_out,
+    tok, wv, rows, own, dhs, dhr, wall, acc, dwv, mb, rk, gt, scs, scr,
+    loc, x_sem, m_send, m_recv, z_up, z_dn, z_recv, c_send, c_recv, d_send, d_recv,
+    w_send, w_recv, s_send, s_recv, o_sem,
+):
+    half = wv.shape[0]
+    cap = gpre.shape[3]
+    e = lax.axis_index("expert")
+    x = lax.axis_index("dp")
+    z, c = e // 2, e % 2
+    ox = 1 - x
+    sib = 2 * z + 1 - c
+    hid = wv.shape[1]
+
+    def remote(src, dst, ss, rs, ee, xx):
+        return pltpu.make_async_remote_copy(
+            src_ref=src, dst_ref=dst, send_sem=ss, recv_sem=rs,
+            device_id={"expert": ee, "dp": xx}, device_id_type=pl.DeviceIdType.MESH,
+        )
+
+    def order(k):
+        inner = jnp.where(k == 0, 1, jnp.where(k == 1, 0, k))
+        low = jnp.where((z == 1) | (z == 2), inner, k)
+        return jnp.where(z < 2, low, 3 - low)
+
+    mine = gout.at[:, pl.ds(pl.multiple_of(x * half, 128), half)]
+    other = gout.at[:, pl.ds(pl.multiple_of(ox * half, 128), half)]
+    tok_copy = pltpu.make_async_copy(mine, tok.at[e, 0], loc.at[0])
+    w_copy = pltpu.make_async_copy(wdn.at[0], wv, loc.at[1])
+    tok_copy.start()
+    w_copy.start()
+    barrier = pltpu.get_barrier_semaphore()
+    peers = [((e + d) % 8, x, 0, e, (e + d) % 8) for d in range(1, 8)]
+    peers += [((e + d) % 8, ox, 1, e + 8, (e + d) % 8 + 8) for d in range(8)]
+    for ee, xx, _, _, _ in peers:
+        pl.semaphore_signal(
+            barrier, inc=1, device_id={"expert": ee, "dp": xx},
+            device_id_type=pl.DeviceIdType.MESH,
+        )
+    mb[e] = meta_ref[...]
+    wall[:, 0:2 * PAD, :] = jnp.zeros((4, 2 * PAD, hid), jnp.bfloat16)
+    tok_copy.wait()
+    pl.semaphore_wait(barrier, 15)
+
+    def meta_copy(i):
+        ee, xx, q, slot, _ = peers[i]
+        return remote(meta_ref, mb.at[slot], m_send.at[i], m_recv.at[slot], ee, xx)
+
+    for i in range(15):
+        meta_copy(i).start()
+    x_copy = remote(other, tok.at[e, 1], x_sem.at[0], x_sem.at[1], e, ox)
+    x_copy.start()
+
+    def up(zp, q):
+        t = tok.at[2 * zp + c, q]
+        return remote(t, t, z_up.at[zp, q], z_recv.at[zp, q], e + 2, x)
+
+    def down(zp, q):
+        t = tok.at[2 * zp + c, q]
+        return remote(t, t, z_dn.at[zp, q], z_recv.at[zp, q], e - 2, x)
+
+    def across(zp, q):
+        t = tok.at[2 * zp + c, q]
+        return remote(t, t, c_send.at[zp, q], c_recv.at[zp, q], sib, x)
+
+    def arrived(zp, q):
+        t = tok.at[2 * zp + c, q]
+        remote(t, t, z_up.at[zp, q], z_recv.at[zp, q], e, ox).wait_recv()
+
+    def sibling(zp, q):
+        t = tok.at[2 * zp + 1 - c, q]
+        remote(t, t, c_send.at[zp, q], c_recv.at[zp, q], sib, x).wait_recv()
+
+    def forward(zp, q):
+        @pl.when((zp <= z) & (z < 3))
+        def _():
+            up(zp, q).start()
+
+        @pl.when((zp >= z) & (z > 0))
+        def _():
+            down(zp, q).start()
+
+        across(zp, q).start()
+
+    forward(z, 0)
+
+    for i in range(15):
+        ee, xx, q, _, slot = peers[i]
+        remote(meta_ref, mb.at[slot], m_send.at[i], m_recv.at[slot], ee, xx).wait_recv()
+
+    named = (mb[:, 0:4, :] == e.astype(jnp.float32)).astype(jnp.float32)
+    hit = jnp.sum(named, axis=1)
+    gt[...] = jnp.sum(named * mb[:, 4:8, :], axis=1)
+    before = (
+        lax.broadcasted_iota(jnp.int32, (128, 128), 0)
+        < lax.broadcasted_iota(jnp.int32, (128, 128), 1)
+    )
+    rank = jnp.dot(
+        hit.astype(jnp.bfloat16), before.astype(jnp.float32).astype(jnp.bfloat16),
+        preferred_element_type=jnp.float32,
+    )
+    rk[...] = jnp.where(hit > 0.5, rank, -1.0)
+    slot_id = lax.broadcasted_iota(jnp.int32, (PAD, 128), 0).astype(jnp.float32)
+
+    def placer(b):
+        return (slot_id == rk[pl.ds(b, 1), :]).astype(jnp.float32)
+
+    def w_copy_out(zp):
+        return remote(
+            wall.at[zp, 0:2 * PAD], wall.at[zp, 2 * PAD:4 * PAD],
+            w_send.at[zp], w_recv.at[zp], e, ox,
+        )
+
+    @pl.loop(0, 4)
+    def _(k):
+        zp = order(k)
+        for cc in range(2):
+            s = 2 * zp + cc
+            place = placer(s)
+            gate = jnp.sum(place * gt[pl.ds(s, 1), :], axis=1, keepdims=True)[0:cap]
+            a = gpre[0, 0, s].astype(jnp.float32)
+            u = upre[0, 0, s].astype(jnp.float32)
+            wall[zp, cc * PAD:cc * PAD + cap, :] = (
+                gate * (a * jax.nn.sigmoid(a) * u)
+            ).astype(jnp.bfloat16)
+        w_copy_out(zp).start()
+
+    acc[...] = jnp.zeros_like(acc)
+    w_copy.wait()
+
+    def dh_copy(zp):
+        return remote(dhs.at[zp], dhr.at[zp], d_send.at[zp], d_recv.at[zp], e, ox)
+
+    def score_copy(s):
+        return remote(scs.at[s], scr.at[e], s_send.at[s], s_recv.at[e], s, x)
+
+    def finish(zp, last):
+        w_copy_out(zp).wait_recv()
+
+        @pl.loop(0, half // TILE)
+        def _(t):
+            at = pl.ds(pl.multiple_of(t * TILE, TILE), TILE)
+            total = acc[at, :] + lax.dot_general(
+                rows[:, at], wall[zp], (((0,), (0,)), ((), ())),
+                preferred_element_type=jnp.float32,
+            )
+            if last:
+                dwv[at, :] = total.astype(jnp.bfloat16)
+                pltpu.make_async_copy(dwv.at[at, :], dw_out.at[0, at, :], o_sem.at[t]).start()
+            else:
+                acc[at, :] = total
+
+        dh_copy(zp).wait_recv()
+        for cc in range(2):
+            s = 2 * zp + cc
+            place = placer(s)
+            gate = jnp.sum(place * gt[pl.ds(s, 1), :], axis=1, keepdims=True)[0:cap]
+            a = gpre[0, 0, s].astype(jnp.float32)
+            u = upre[0, 0, s].astype(jnp.float32)
+            dh = (own[cc] + dhr[zp, cc * PAD:(cc + 1) * PAD, :].astype(jnp.float32))
+            dh = dh[0:cap]
+            sig = jax.nn.sigmoid(a)
+            act = a * sig
+            score = jnp.sum(dh * (act * u), axis=1, keepdims=True)
+            d_act = gate * dh
+            da_ref[0, 0, s] = (d_act * u * sig * (1.0 + a * (1.0 - sig))).astype(jnp.bfloat16)
+            du_ref[0, 0, s] = (d_act * act).astype(jnp.bfloat16)
+            by_token = jnp.sum(place[0:cap] * score, axis=0, keepdims=True)
+            full = jnp.broadcast_to(by_token, (8, 128))
+
+            @pl.when(s == e)
+            def _():
+                scr[e] = full
+
+            @pl.when(s != e)
+            def _():
+                scs[s] = full
+                score_copy(s).start()
+
+    @pl.loop(0, 4)
+    def _(k):
+        zp = order(k)
+
+        @pl.when(k > 0)
+        def _():
+            arrived(zp, 0)
+            forward(zp, 0)
+            finish(order(k - 1), False)
+            arrived(zp, 1)
+
+        @pl.when(k == 0)
+        def _():
+            x_copy.wait_recv()
+
+        forward(zp, 1)
+        sibling(zp, 0)
+        sibling(zp, 1)
+        for q in (1, 0):
+            for cc in range(2):
+                s = 2 * zp + cc
+                j = (q * 2 + cc) * PAD
+                rows[j:j + PAD, :] = jnp.dot(
+                    placer(q * 8 + s).astype(jnp.bfloat16), tok[s, q],
+                    preferred_element_type=jnp.float32,
+                ).astype(jnp.bfloat16)
+            part = jnp.dot(
+                rows[q * 2 * PAD:(q + 1) * 2 * PAD, :], wv[...],
+                preferred_element_type=jnp.float32,
+            )
+            if q == 1:
+                dhs[zp] = part.astype(jnp.bfloat16)
+                dh_copy(zp).start()
+            else:
+                own[...] = part.reshape(2, PAD, hid)
+
+    finish(order(3), True)
+
+    for d in range(1, 8):
+        s = (e + d) % 8
+        remote(scs.at[s], scr.at[s], s_send.at[s], s_recv.at[s], s, x).wait_recv()
+    routes = meta_ref[0:4, :]
+    total = jnp.zeros((4, 128), jnp.float32)
+    for i in range(8):
+        total += jnp.where(routes == float(i), scr[i, 0:1, :], 0.0)
+    dg_ref[...] = total
+
+    x_copy.wait_send()
+    for i in range(15):
+        meta_copy(i).wait_send()
+    for zp in range(4):
+        for q in range(2):
+            @pl.when((zp <= z) & (z < 3))
+            def _():
+                up(zp, q).wait_send()
+
+            @pl.when((zp >= z) & (z > 0))
+            def _():
+                down(zp, q).wait_send()
+
+            across(zp, q).wait_send()
+        dh_copy(zp).wait_send()
+        w_copy_out(zp).wait_send()
+    for d in range(1, 8):
+        score_copy((e + d) % 8).wait_send()
+    for t in range(half // TILE):
+        at = pl.ds(t * TILE, TILE)
+        pltpu.make_async_copy(dwv.at[at, :], dw_out.at[0, at, :], o_sem.at[t]).wait()
+
+
+def local_kernel(grad_out, routes, gates, gate_pre, up_pre, w_down):
+    half, hid = w_down.shape[1], w_down.shape[2]
+    meta = jnp.concatenate(
+        [routes.astype(jnp.float32), gates.astype(jnp.float32)], axis=1
+    ).T
+    vmem = pl.BlockSpec(memory_space=pltpu.VMEM)
+    hbm = pl.BlockSpec(memory_space=pl.ANY)
+    dma = pltpu.SemaphoreType.DMA
+    bf, f4 = jnp.bfloat16, jnp.float32
+    dg, d_a, d_u, d_w = pl.pallas_call(
+        whole_kernel,
+        out_shape=(
+            jax.ShapeDtypeStruct((4, 128), f4),
+            jax.ShapeDtypeStruct(gate_pre.shape, bf),
+            jax.ShapeDtypeStruct(up_pre.shape, bf),
+            jax.ShapeDtypeStruct(w_down.shape, bf),
+        ),
+        in_specs=[vmem, hbm, vmem, vmem, hbm],
+        out_specs=(vmem, vmem, vmem, hbm),
+        scratch_shapes=[
+            pltpu.VMEM((8, 2, 128, half), bf),
+            pltpu.VMEM((half, hid), bf),
+            pltpu.VMEM((4 * PAD, half), bf),
+            pltpu.VMEM((2, PAD, hid), f4),
+            pltpu.VMEM((4, 2 * PAD, hid), bf),
+            pltpu.VMEM((4, 2 * PAD, hid), bf),
+            pltpu.VMEM((4, 4 * PAD, hid), bf),
+            pltpu.VMEM((half, hid), f4),
+            pltpu.VMEM((half, hid), bf),
+            pltpu.VMEM((16, 8, 128), f4),
+            pltpu.VMEM((16, 128), f4),
+            pltpu.VMEM((16, 128), f4),
+            pltpu.VMEM((8, 8, 128), f4),
+            pltpu.VMEM((8, 8, 128), f4),
+            dma((2,)), dma((2,)), dma((15,)), dma((16,)),
+            dma((4, 2)), dma((4, 2)), dma((4, 2)), dma((4, 2)), dma((4, 2)),
+            dma((4,)), dma((4,)), dma((4,)), dma((4,)),
+            dma((8,)), dma((8,)), dma((half // TILE,)),
+        ],
+        compiler_params=pltpu.CompilerParams(
+            collective_id=0, has_side_effects=True, vmem_limit_bytes=56 * 1024 * 1024
+        ),
+    )(meta, grad_out, gate_pre, up_pre, w_down)
+    return (dg.T, d_a, d_u, d_w)
 
 
 def local(grad_out, routes, gates, gate_pre, up_pre, w_down):
@@ -98,8 +400,10 @@
         P(("groups", "expert"), "dp", None, None, "node"),
         P("expert", "dp", "node"),
     )
+    sizes = dict(mesh.shape)
+    small = (sizes["expert"], sizes["dp"], sizes["node"]) == (8, 2, 1)
     return jax.shard_map(
-        local,
+        local_kernel if small else local,
         mesh=mesh,
         in_specs=placed,
         out_specs=(

time: 236 us -> 128 us (0.54)
  waiting for transfers between devices: 153 us -> 0 us
  Pallas kernels: 0 us -> 114 us
  matrix products: 23.2 us -> 0 us
  local copies, waits for them, and re-layouts: 26.6 us -> 11.2 us
  starting transfers between devices: 14.9 us -> 0 us
  between operations: 14.2 us -> 0.66 us
    pallas_call x0 -> x1, Pallas kernels: none -> 114 us  [local_kernel(): pl.pallas_call(whole_kernel, out_shape=(jax.ShapeDtypeStruct((4, 128), f4...]
    all_to_all x3 -> x0, waiting for transfers between devices: 104 us -> none  [the longest x1 102 us: local(): lax.all_to_all(pair_rows, 'expert', split_axis=1, concat_axis=0, tiled=True)]
    reduce_scatter x1 -> x0, waiting for transfers between devices: 48.2 us -> none  [local(): lax.psum_scatter(lax.dot_general(columns, weighted, (((0,), (0,)), ((), (...]
    dot_general x4 -> x0, matrix products: 23.2 us -> none  [the longest x1 10.2 us: local(): jnp.dot(columns, lax.all_gather(w_down, 'dp', axis=1, tiled=True)[0], pre...]
    all_to_all x3 -> x0, starting transfers between devices: 14.8 us -> none  [the longest x1 6.33 us: local(): lax.all_to_all(pair_gates, 'expert', split_axis=1, concat_axis=0, tiled=T...]
    reshape x6 -> x0, local copies, waits for them, and re-layouts: 7.52 us -> none  [the longest x1 5.21 us: local(): rows = recv_rows.reshape(slot_count, width)]
    unnamed x14 -> x10, local copies, waits for them, and re-layouts: 4.28 us -> 11.2 us
    convert_element_type x8 -> x0, local copies, waits for them, and re-layouts: 6.94 us -> none  [the longest x2 4.04 us: local(): pre_a = gate_pre.reshape(slot_count, hidden).astype(jnp.float32)]
  transfers between devices with their start and end apart: 5 -> 0, of which waited for: 3 -> 0; matrix products, arithmetic and copies ran while one was open for 21% -> 0% of each run, Pallas kernels for 0% -> 0%
where the time goes in v1:
time: 128 us
  Pallas kernels  114 us (89%)
  local copies, waits for them, and re-layouts  11.2 us (9%)
  other arithmetic  1.97 us (2%)
    pallas_call x1, Pallas kernels, local_kernel(): pl.pallas_call(whole_kernel, out_shape=(jax.ShapeDtypeStruct((4, 128), f4...  114 us
    unnamed x10, local copies, waits for them, and re-layouts  11.2 us

profile of v1, /device:TPU:0, one launch (start us, length us, event | category | flops | bytes accessed | tf_op | source)
XLA Modules:
  0.0 128.0 jit_solution(10738185439692231170)
XLA Ops:
  0.6 0.7 convert_element_type.6
  1.3 0.7 convert_element_type.7
  2.0 0.6 maximum_bitcast_fusion.meta_ref
  2.6 2.2 %copy.10.gpre = bf16[1,1,8,68,768]{4,3,2,1,0:T(8,128)(2,1)} copy(bf16[1,1,8,68,768]{4,2,3,1,0:T(8,128)(2,1)} %param.9) | data formatting | bytes 1671168 | tf_op args[3]
  4.8 2.2 %copy.11.upre = bf16[1,1,8,68,768]{4,3,2,1,0:T(8,128)(2,1)} copy(bf16[1,1,8,68,768]{4,2,3,1,0:T(8,128)(2,1)} %param.10) | data formatting | bytes 1671168 | tf_op args[4]
  7.0 114.2 %shard_map.93 = (f32[4,128]{1,0:T(4,128)}, bf16[1,1,8,68,768]{4,3,2,1,0:T(8,128)(2,1)}, bf16[1,1,8,68,768]{4,3,2,1,0:T(8,128)(2,1)}, bf16[1,2048,768]{2,1,0:T(8,128)(2,1)}) custom-call(f32[8,128]{1,0:T(8,128)} %maximum_bitcast_fusion.meta_ref, bf16[128,4096]{1,0:T(8,128)(2,1)} %gout.1, bf16[1,1,8,68,768]{4,3,2,1,0:T(8,128)(2,1)} %copy.10.gpre, ...), custom_call_target="tpu_custom_call" | custom-call | tf_op jit(solution)/shard_map/pallas_call | solution.py:272
  121.2 0.0 copy-start.1
  121.2 0.0 copy-start
  121.2 2.4 %copy.12 = bf16[1,1,8,68,768]{4,2,3,1,0:T(8,128)(2,1)} copy(bf16[1,1,8,68,768]{4,3,2,1,0:T(8,128)(2,1)} %get-tuple-element.13) | data formatting | bytes 1671168
  123.6 2.2 %copy.13 = bf16[1,1,8,68,768]{4,2,3,1,0:T(8,128)(2,1)} copy(bf16[1,1,8,68,768]{4,3,2,1,0:T(8,128)(2,1)} %get-tuple-element.14) | data formatting | bytes 1671168
  125.8 0.0 copy-done.1
  125.8 0.6 copy.16
  126.4 0.0 copy-done
  126.4 1.7 %copy.17 = bf16[1,2048,768]{2,1,0:T(8,128)(2,1)} copy(bf16[1,2048,768]{2,1,0:T(8,128)(2,1)S(1)} %copy-done) | data formatting | bytes 6291456
Async XLA Ops:
  121.2 4.6 %copy-start.1 = (f32[4,128]{1,0:T(4,128)S(1)}, f32[4,128]{1,0:T(4,128)}, u32[]{:S(2)}) copy-start(f32[4,128]{1,0:T(4,128)} %get-tuple-element.8) | copy-start | bytes 6148
  121.2 5.2 %copy-start = (bf16[1,2048,768]{2,1,0:T(8,128)(2,1)S(1)}, bf16[1,2048,768]{2,1,0:T(8,128)(2,1)}, u32[]{:S(2)}) copy-start(bf16[1,2048,768]{2,1,0:T(8,128)(2,1)} %get-tuple-element.23) | copy-start | bytes 9437188

commit v2 on v1

--- a/solution.py
+++ b/solution.py
@@ -11,19 +11,29 @@
 
 
 def whole_kernel(
-    meta_ref, gout, gpre, upre, wdn, dg_ref, da_ref, du_ref, dw_out,
-    tok, wv, rows, own, dhs, dhr, wall, acc, dwv, mb, rk, gt, scs, scr,
+    routes_ref, gates_ref, gout, gpre, upre, wdn, dg_ref, da_ref, du_ref, dw_out,
+    meta_ref, a32, u32, tok, wv, rows, own, dhs, dhr, wall, acc, dwv, mb, rk, gt, scs, scr,
     loc, x_sem, m_send, m_recv, z_up, z_dn, z_recv, c_send, c_recv, d_send, d_recv,
     w_send, w_recv, s_send, s_recv, o_sem,
 ):
     half = wv.shape[0]
-    cap = gpre.shape[3]
+    cap, src = gpre.shape[0], gpre.shape[1]
     e = lax.axis_index("expert")
     x = lax.axis_index("dp")
     z, c = e // 2, e % 2
     ox = 1 - x
     sib = 2 * z + 1 - c
     hid = wv.shape[1]
+    lanes = hid // 128
+
+    def take(ref, s):
+        return jnp.concatenate(
+            [ref[h, pl.ds(s, cap, stride=src), :] for h in range(lanes)], axis=1
+        )
+
+    def put(ref, s, value):
+        for h in range(lanes):
+            ref[h, pl.ds(s, cap, stride=src), :] = value[:, h * 128:h * 128 + 128]
 
     def remote(src, dst, ss, rs, ee, xx):
         return pltpu.make_async_remote_copy(
@@ -50,6 +60,8 @@
             barrier, inc=1, device_id={"expert": ee, "dp": xx},
             device_id_type=pl.DeviceIdType.MESH,
         )
+    meta_ref[0:4, :] = routes_ref[...].astype(jnp.float32)
+    meta_ref[4:8, :] = gates_ref[...].astype(jnp.float32)
     mb[e] = meta_ref[...]
     wall[:, 0:2 * PAD, :] = jnp.zeros((4, 2 * PAD, hid), jnp.bfloat16)
     tok_copy.wait()
@@ -96,6 +108,10 @@
         across(zp, q).start()
 
     forward(z, 0)
+    for h in range(lanes):
+        at = slice(h * 128, h * 128 + 128)
+        a32[h] = gpre[:, :, at].astype(jnp.float32).reshape(cap * src, 128)
+        u32[h] = upre[:, :, at].astype(jnp.float32).reshape(cap * src, 128)
 
     for i in range(15):
         ee, xx, q, _, slot = peers[i]
@@ -131,14 +147,17 @@
             s = 2 * zp + cc
             place = placer(s)
             gate = jnp.sum(place * gt[pl.ds(s, 1), :], axis=1, keepdims=True)[0:cap]
-            a = gpre[0, 0, s].astype(jnp.float32)
-            u = upre[0, 0, s].astype(jnp.float32)
+            a = take(a32, s)
+            u = take(u32, s)
             wall[zp, cc * PAD:cc * PAD + cap, :] = (
                 gate * (a * jax.nn.sigmoid(a) * u)
             ).astype(jnp.bfloat16)
-        w_copy_out(zp).start()
 
     acc[...] = jnp.zeros_like(acc)
+    x_copy.wait_recv()
+    forward(z, 1)
+    for k in range(4):
+        w_copy_out(order(k)).start()
     w_copy.wait()
 
     def dh_copy(zp):
@@ -168,16 +187,16 @@
             s = 2 * zp + cc
             place = placer(s)
             gate = jnp.sum(place * gt[pl.ds(s, 1), :], axis=1, keepdims=True)[0:cap]
-            a = gpre[0, 0, s].astype(jnp.float32)
-            u = upre[0, 0, s].astype(jnp.float32)
+            a = take(a32, s)
+            u = take(u32, s)
             dh = (own[cc] + dhr[zp, cc * PAD:(cc + 1) * PAD, :].astype(jnp.float32))
             dh = dh[0:cap]
             sig = jax.nn.sigmoid(a)
             act = a * sig
             score = jnp.sum(dh * (act * u), axis=1, keepdims=True)
             d_act = gate * dh
-            da_ref[0, 0, s] = (d_act * u * sig * (1.0 + a * (1.0 - sig))).astype(jnp.bfloat16)
-            du_ref[0, 0, s] = (d_act * act).astype(jnp.bfloat16)
+            put(a32, s, d_act * u * sig * (1.0 + a * (1.0 - sig)))
+            put(u32, s, d_act * act)
             by_token = jnp.sum(place[0:cap] * score, axis=0, keepdims=True)
             full = jnp.broadcast_to(by_token, (8, 128))
 
@@ -190,22 +209,51 @@
                 scs[s] = full
                 score_copy(s).start()
 
+    def relay(d, q):
+        @pl.when(z >= d)
+        def _():
+            arrived(z - d, q)
+            forward(z - d, q)
+
+        @pl.when(z + d < 4)
+        def _():
+            arrived(z + d, q)
+            forward(z + d, q)
+
     @pl.loop(0, 4)
     def _(k):
         zp = order(k)
+        end = (z == 0) | (z == 3)
+
+        @pl.when(k == 0)
+        def _():
+            relay(1, 0)
+
+        @pl.when(k == 1)
+        def _():
+            relay(1, 1)
+
+        @pl.when(k == 2)
+        def _():
+            relay(2, 0)
+
+        @pl.when((k == 3) & (z > 0) & (z < 3))
+        def _():
+            relay(2, 1)
 
         @pl.when(k > 0)
         def _():
-            arrived(zp, 0)
-            forward(zp, 0)
             finish(order(k - 1), False)
-            arrived(zp, 1)
-
-        @pl.when(k == 0)
-        def _():
-            x_copy.wait_recv()
-
-        forward(zp, 1)
+
+        @pl.when((k == 2) & end)
+        def _():
+            relay(2, 1)
+
+        @pl.when((k == 3) & end)
+        def _():
+            relay(3, 0)
+            relay(3, 1)
+
         sibling(zp, 0)
         sibling(zp, 1)
         for q in (1, 0):
@@ -227,6 +275,10 @@
                 own[...] = part.reshape(2, PAD, hid)
 
     finish(order(3), True)
+    for h in range(lanes):
+        at = slice(h * 128, h * 128 + 128)
+        da_ref[:, :, at] = a32[h].reshape(cap, src, 128).astype(jnp.bfloat16)
+        du_ref[:, :, at] = u32[h].reshape(cap, src, 128).astype(jnp.bfloat16)
 
     for d in range(1, 8):
         s = (e + d) % 8
@@ -262,9 +314,8 @@
 
 def local_kernel(grad_out, routes, gates, gate_pre, up_pre, w_down):
     half, hid = w_down.shape[1], w_down.shape[2]
-    meta = jnp.concatenate(
-        [routes.astype(jnp.float32), gates.astype(jnp.float32)], axis=1
-    ).T
+    cap, src = gate_pre.shape[3], gate_pre.shape[2]
+    slots = (cap, src, hid)
     vmem = pl.BlockSpec(memory_space=pltpu.VMEM)
     hbm = pl.BlockSpec(memory_space=pl.ANY)
     dma = pltpu.SemaphoreType.DMA
@@ -273,13 +324,16 @@
         whole_kernel,
         out_shape=(
             jax.ShapeDtypeStruct((4, 128), f4),
-            jax.ShapeDtypeStruct(gate_pre.shape, bf),
-            jax.ShapeDtypeStruct(up_pre.shape, bf),
+            jax.ShapeDtypeStruct(slots, bf),
+            jax.ShapeDtypeStruct(slots, bf),
             jax.ShapeDtypeStruct(w_down.shape, bf),
         ),
-        in_specs=[vmem, hbm, vmem, vmem, hbm],
+        in_specs=[vmem, vmem, hbm, vmem, vmem, hbm],
         out_specs=(vmem, vmem, vmem, hbm),
         scratch_shapes=[
+            pltpu.VMEM((8, 128), f4),
+            pltpu.VMEM((hid // 128, cap * src, 128), f4),
+            pltpu.VMEM((hid // 128, cap * src, 128), f4),
             pltpu.VMEM((8, 2, 128, half), bf),
             pltpu.VMEM((half, hid), bf),
             pltpu.VMEM((4 * PAD, half), bf),
@@ -302,7 +356,11 @@
         compiler_params=pltpu.CompilerParams(
             collective_id=0, has_side_effects=True, vmem_limit_bytes=56 * 1024 * 1024
         ),
-    )(meta, grad_out, gate_pre, up_pre, w_down)
+    )(
+        routes.T, gates.T, grad_out,
+        jnp.swapaxes(gate_pre[0, 0], 0, 1), jnp.swapaxes(up_pre[0, 0], 0, 1), w_down,
+    )
+    d_a, d_u = (jnp.swapaxes(v, 0, 1)[None, None] for v in (d_a, d_u))
     return (dg.T, d_a, d_u, d_w)
 
 

time: 128 us -> 102 us (0.80)
  Pallas kernels: 114 us -> 93.4 us
  local copies, waits for them, and re-layouts: 11.2 us -> 7.28 us
  other arithmetic: 1.97 us -> 0 us
    pallas_call x1, Pallas kernels: 114 us -> 93.4 us  [local_kernel(): pl.pallas_call(whole_kernel, out_shape=(jax.ShapeDtypeStruct((4, 128), f4...]
    unnamed x10 -> x6, local copies, waits for them, and re-layouts: 11.2 us -> 7.28 us
    convert_element_type x2 -> x0, other arithmetic: 1.37 us -> none  [the longest x1 0.68 us: local_kernel(): routes.astype(jnp.float32)]
where the time goes in v2:
time: 102 us; the launch traced here: 101 us
  Pallas kernels  93.4 us (92%)
  local copies, waits for them, and re-layouts  7.28 us (7%)
    pallas_call x1, Pallas kernels, local_kernel(): pl.pallas_call(whole_kernel, out_shape=(jax.ShapeDtypeStruct((4, 128), f4...  93.4 us
    unnamed x6, local copies, waits for them, and re-layouts  7.28 us

profile of v2, /device:TPU:0, one launch (start us, length us, event | category | flops | bytes accessed | tf_op | source)
XLA Modules:
  0.0 101.4 jit_solution(4840579168774490197)
XLA Ops:
  0.6 93.4 %shard_map.93 = (f32[4,128]{1,0:T(4,128)}, bf16[68,8,768]{2,1,0:T(8,128)(2,1)}, bf16[68,8,768]{2,1,0:T(8,128)(2,1)}, bf16[1,2048,768]{2,1,0:T(8,128)(2,1)}) custom-call(s32[4,128]{1,0:T(4,128)} %bitcast.19, bf16[4,128]{1,0:T(4,128)(2,1)} %bitcast.21, bf16[128,4096]{1,0:T(8,128)(2,1)} %gout.1, bf16[68,8,768]{2,1,0:T(8,128)(2,1)} %bitcast.17, ...), custom_call_target="tpu_custom_call" | custom-call | tf_op jit(solution)/shard_map/pallas_call | solution.py:323
  94.1 0.0 copy-start
  94.1 1.4 %copy.14 = f32[128,4]{0,1:T(4,128)} copy(f32[128,4]{0,1:T(4,128)} %bitcast.20) | data formatting | bytes 4096
  95.5 2.1 %copy.15 = bf16[1,1,8,68,768]{4,2,3,1,0:T(8,128)(2,1)} copy(bf16[1,1,8,68,768]{4,2,3,1,0:T(8,128)(2,1)} %bitcast.16) | data formatting | bytes 1671168
  97.6 2.1 %copy.16 = bf16[1,1,8,68,768]{4,2,3,1,0:T(8,128)(2,1)} copy(bf16[1,1,8,68,768]{4,2,3,1,0:T(8,128)(2,1)} %bitcast.15) | data formatting | bytes 1671168
  99.7 0.0 copy-done
  99.7 1.7 %copy.17 = bf16[1,2048,768]{2,1,0:T(8,128)(2,1)} copy(bf16[1,2048,768]{2,1,0:T(8,128)(2,1)S(1)} %copy-done) | data formatting | bytes 6291456
Async XLA Ops:
  94.1 5.6 %copy-start = (bf16[1,2048,768]{2,1,0:T(8,128)(2,1)S(1)}, bf16[1,2048,768]{2,1,0:T(8,128)(2,1)}, u32[]{:S(2)}) copy-start(bf16[1,2048,768]{2,1,0:T(8,128)(2,1)} %get-tuple-element.19) | copy-start | bytes 9437188

commit v3 on v2

--- a/solution.py
+++ b/solution.py
@@ -47,7 +47,6 @@
         return jnp.where(z < 2, low, 3 - low)
 
     mine = gout.at[:, pl.ds(pl.multiple_of(x * half, 128), half)]
-    other = gout.at[:, pl.ds(pl.multiple_of(ox * half, 128), half)]
     tok_copy = pltpu.make_async_copy(mine, tok.at[e, 0], loc.at[0])
     w_copy = pltpu.make_async_copy(wdn.at[0], wv, loc.at[1])
     tok_copy.start()
@@ -73,27 +72,36 @@
 
     for i in range(15):
         meta_copy(i).start()
-    x_copy = remote(other, tok.at[e, 1], x_sem.at[0], x_sem.at[1], e, ox)
-    x_copy.start()
+    part_w = half // 2
+
+    def x_copy(r):
+        src = gout.at[:, pl.ds(pl.multiple_of(ox * half + r * part_w, 128), part_w)]
+        return remote(src, unit(e, 2 + r), x_sem.at[r], x_sem.at[2 + r], e, ox)
+
+    def unit(s, r):
+        return tok.at[s, r // 2, :, r % 2 * part_w:(r % 2 + 1) * part_w]
+
+    x_copy(0).start()
+    x_copy(1).start()
 
     def up(zp, q):
-        t = tok.at[2 * zp + c, q]
+        t = unit(2 * zp + c, q)
         return remote(t, t, z_up.at[zp, q], z_recv.at[zp, q], e + 2, x)
 
     def down(zp, q):
-        t = tok.at[2 * zp + c, q]
+        t = unit(2 * zp + c, q)
         return remote(t, t, z_dn.at[zp, q], z_recv.at[zp, q], e - 2, x)
 
     def across(zp, q):
-        t = tok.at[2 * zp + c, q]
+        t = unit(2 * zp + c, q)
         return remote(t, t, c_send.at[zp, q], c_recv.at[zp, q], sib, x)
 
     def arrived(zp, q):
-        t = tok.at[2 * zp + c, q]
+        t = unit(2 * zp + c, q)
         remote(t, t, z_up.at[zp, q], z_recv.at[zp, q], e, ox).wait_recv()
 
     def sibling(zp, q):
-        t = tok.at[2 * zp + 1 - c, q]
+        t = unit(2 * zp + 1 - c, q)
         remote(t, t, c_send.at[zp, q], c_recv.at[zp, q], sib, x).wait_recv()
 
     def forward(zp, q):
@@ -108,6 +116,7 @@
         across(zp, q).start()
 
     forward(z, 0)
+    forward(z, 1)
     for h in range(lanes):
         at = slice(h * 128, h * 128 + 128)
         a32[h] = gpre[:, :, at].astype(jnp.float32).reshape(cap * src, 128)
@@ -154,8 +163,9 @@
             ).astype(jnp.bfloat16)
 
     acc[...] = jnp.zeros_like(acc)
-    x_copy.wait_recv()
-    forward(z, 1)
+    for r in range(2):
+        x_copy(r).wait_recv()
+        forward(z, 2 + r)
     for k in range(4):
         w_copy_out(order(k)).start()
     w_copy.wait()
@@ -228,10 +238,12 @@
         @pl.when(k == 0)
         def _():
             relay(1, 0)
+            relay(1, 1)
 
         @pl.when(k == 1)
         def _():
-            relay(1, 1)
+            relay(1, 2)
+            relay(1, 3)
 
         @pl.when(k == 2)
         def _():
@@ -239,6 +251,8 @@
 
         @pl.when((k == 3) & (z > 0) & (z < 3))
         def _():
+            relay(2, 2)
+            relay(2, 3)
             relay(2, 1)
 
         @pl.when(k > 0)
@@ -247,16 +261,24 @@
 
         @pl.when((k == 2) & end)
         def _():
+            relay(2, 2)
+            relay(2, 3)
             relay(2, 1)
 
         @pl.when((k == 3) & end)
         def _():
             relay(3, 0)
-            relay(3, 1)
-
-        sibling(zp, 0)
-        sibling(zp, 1)
+            relay(3, 2)
+            relay(3, 3)
+
         for q in (1, 0):
+            if q == 0:
+                @pl.when((k == 3) & end)
+                def _():
+                    relay(3, 1)
+
+            sibling(zp, 2 * q)
+            sibling(zp, 2 * q + 1)
             for cc in range(2):
                 s = 2 * zp + cc
                 j = (q * 2 + cc) * PAD
@@ -289,11 +311,12 @@
         total += jnp.where(routes == float(i), scr[i, 0:1, :], 0.0)
     dg_ref[...] = total
 
-    x_copy.wait_send()
+    x_copy(0).wait_send()
+    x_copy(1).wait_send()
     for i in range(15):
         meta_copy(i).wait_send()
     for zp in range(4):
-        for q in range(2):
+        for q in range(4):
             @pl.when((zp <= z) & (z < 3))
             def _():
                 up(zp, q).wait_send()
@@ -348,8 +371,8 @@
             pltpu.VMEM((16, 128), f4),
             pltpu.VMEM((8, 8, 128), f4),
             pltpu.VMEM((8, 8, 128), f4),
-            dma((2,)), dma((2,)), dma((15,)), dma((16,)),
-            dma((4, 2)), dma((4, 2)), dma((4, 2)), dma((4, 2)), dma((4, 2)),
+            dma((2,)), dma((4,)), dma((15,)), dma((16,)),
+            dma((4, 4)), dma((4, 4)), dma((4, 4)), dma((4, 4)), dma((4, 4)),
             dma((4,)), dma((4,)), dma((4,)), dma((4,)),
             dma((8,)), dma((8,)), dma((half // TILE,)),
         ],

time: 102 us -> 96.4 us (0.945)
  Pallas kernels: 93.4 us -> 88.2 us
    pallas_call x1, Pallas kernels: 93.4 us -> 88.2 us  [local_kernel(): pl.pallas_call(whole_kernel, out_shape=(jax.ShapeDtypeStruct((4, 128), f4...]
where the time goes in v3:
time: 96.4 us; the launch traced here: 96.2 us
  Pallas kernels  88.2 us (91%)
  local copies, waits for them, and re-layouts  7.28 us (8%)
    pallas_call x1, Pallas kernels, local_kernel(): pl.pallas_call(whole_kernel, out_shape=(jax.ShapeDtypeStruct((4, 128), f4...  88.2 us
    unnamed x6, local copies, waits for them, and re-layouts  7.28 us

profile of v3, /device:TPU:0, one launch (start us, length us, event | category | flops | bytes accessed | tf_op | source)
XLA Modules:
  0.0 96.2 jit_solution(10518126845157425992)
XLA Ops:
  0.6 88.2 %shard_map.93 = (f32[4,128]{1,0:T(4,128)}, bf16[68,8,768]{2,1,0:T(8,128)(2,1)}, bf16[68,8,768]{2,1,0:T(8,128)(2,1)}, bf16[1,2048,768]{2,1,0:T(8,128)(2,1)}) custom-call(s32[4,128]{1,0:T(4,128)} %bitcast.19, bf16[4,128]{1,0:T(4,128)(2,1)} %bitcast.21, bf16[128,4096]{1,0:T(8,128)(2,1)} %gout.1, bf16[68,8,768]{2,1,0:T(8,128)(2,1)} %bitcast.17, ...), custom_call_target="tpu_custom_call" | custom-call | tf_op jit(solution)/shard_map/pallas_call | solution.py:346
  88.9 0.0 copy-start
  88.9 1.4 %copy.14 = f32[128,4]{0,1:T(4,128)} copy(f32[128,4]{0,1:T(4,128)} %bitcast.20) | data formatting | bytes 4096
  90.3 2.1 %copy.15 = bf16[1,1,8,68,768]{4,2,3,1,0:T(8,128)(2,1)} copy(bf16[1,1,8,68,768]{4,2,3,1,0:T(8,128)(2,1)} %bitcast.16) | data formatting | bytes 1671168
  92.4 2.1 %copy.16 = bf16[1,1,8,68,768]{4,2,3,1,0:T(8,128)(2,1)} copy(bf16[1,1,8,68,768]{4,2,3,1,0:T(8,128)(2,1)} %bitcast.15) | data formatting | bytes 1671168
  94.5 0.0 copy-done
  94.5 1.7 %copy.17 = bf16[1,2048,768]{2,1,0:T(8,128)(2,1)} copy(bf16[1,2048,768]{2,1,0:T(8,128)(2,1)S(1)} %copy-done) | data formatting | bytes 6291456
Async XLA Ops:
  88.9 5.6 %copy-start = (bf16[1,2048,768]{2,1,0:T(8,128)(2,1)S(1)}, bf16[1,2048,768]{2,1,0:T(8,128)(2,1)}, u32[]{:S(2)}) copy-start(bf16[1,2048,768]{2,1,0:T(8,128)(2,1)} %get-tuple-element.19) | copy-start | bytes 9437188

commit v4 on v3

--- a/solution.py
+++ b/solution.py
@@ -11,8 +11,8 @@
 
 
 def whole_kernel(
-    routes_ref, gates_ref, gout, gpre, upre, wdn, dg_ref, da_ref, du_ref, dw_out,
-    meta_ref, a32, u32, tok, wv, rows, own, dhs, dhr, wall, acc, dwv, mb, rk, gt, scs, scr,
+    routes_ref, gates_ref, gout, gpre_hbm, upre_hbm, wdn, dg_ref, da_ref, du_ref, dw_out,
+    gpre, upre, meta_ref, a32, u32, tok, wv, rows, own, dhs, dhr, wall, acc, dwv, mb, rk, gt, scs, scr,
     loc, x_sem, m_send, m_recv, z_up, z_dn, z_recv, c_send, c_recv, d_send, d_recv,
     w_send, w_recv, s_send, s_recv, o_sem,
 ):
@@ -51,6 +51,10 @@
     w_copy = pltpu.make_async_copy(wdn.at[0], wv, loc.at[1])
     tok_copy.start()
     w_copy.start()
+    g_copy = pltpu.make_async_copy(gpre_hbm, gpre, loc.at[2])
+    u_copy = pltpu.make_async_copy(upre_hbm, upre, loc.at[3])
+    g_copy.start()
+    u_copy.start()
     barrier = pltpu.get_barrier_semaphore()
     peers = [((e + d) % 8, x, 0, e, (e + d) % 8) for d in range(1, 8)]
     peers += [((e + d) % 8, ox, 1, e + 8, (e + d) % 8 + 8) for d in range(8)]
@@ -117,6 +121,8 @@
 
     forward(z, 0)
     forward(z, 1)
+    g_copy.wait()
+    u_copy.wait()
     for h in range(lanes):
         at = slice(h * 128, h * 128 + 128)
         a32[h] = gpre[:, :, at].astype(jnp.float32).reshape(cap * src, 128)
@@ -335,6 +341,13 @@
         pltpu.make_async_copy(dwv.at[at, :], dw_out.at[0, at, :], o_sem.at[t]).wait()
 
 
+def place_kernel(dg, d_a, d_u, d_w, dg_out, da_out, du_out, dw_out):
+    dg_out[...] = dg[...]
+    da_out[...] = d_a[...]
+    du_out[...] = d_u[...]
+    dw_out[...] = d_w[...]
+
+
 def local_kernel(grad_out, routes, gates, gate_pre, up_pre, w_down):
     half, hid = w_down.shape[1], w_down.shape[2]
     cap, src = gate_pre.shape[3], gate_pre.shape[2]
@@ -351,9 +364,11 @@
             jax.ShapeDtypeStruct(slots, bf),
             jax.ShapeDtypeStruct(w_down.shape, bf),
         ),
-        in_specs=[vmem, vmem, hbm, vmem, vmem, hbm],
+        in_specs=[vmem, vmem, hbm, hbm, hbm, hbm],
         out_specs=(vmem, vmem, vmem, hbm),
         scratch_shapes=[
+            pltpu.VMEM(slots, bf),
+            pltpu.VMEM(slots, bf),
             pltpu.VMEM((8, 128), f4),
             pltpu.VMEM((hid // 128, cap * src, 128), f4),
             pltpu.VMEM((hid // 128, cap * src, 128), f4),
@@ -371,7 +386,7 @@
             pltpu.VMEM((16, 128), f4),
             pltpu.VMEM((8, 8, 128), f4),
             pltpu.VMEM((8, 8, 128), f4),
-            dma((2,)), dma((4,)), dma((15,)), dma((16,)),
+            dma((4,)), dma((4,)), dma((15,)), dma((16,)),
             dma((4, 4)), dma((4, 4)), dma((4, 4)), dma((4, 4)), dma((4, 4)),
             dma((4,)), dma((4,)), dma((4,)), dma((4,)),
             dma((8,)), dma((8,)), dma((half // TILE,)),
@@ -383,6 +398,21 @@
         routes.T, gates.T, grad_out,
         jnp.swapaxes(gate_pre[0, 0], 0, 1), jnp.swapaxes(up_pre[0, 0], 0, 1), w_down,
     )
+    steps = 4
+    specs = (
+        pl.BlockSpec((4, 128), lambda i: (0, 0)),
+        pl.BlockSpec((cap // steps, src, hid), lambda i: (i, 0, 0)),
+        pl.BlockSpec((cap // steps, src, hid), lambda i: (i, 0, 0)),
+        pl.BlockSpec((1, half // steps, hid), lambda i: (0, i, 0)),
+    )
+    dg, d_a, d_u, d_w = pl.pallas_call(
+        place_kernel,
+        grid=(steps,),
+        out_shape=tuple(jax.ShapeDtypeStruct(v.shape, v.dtype) for v in (dg, d_a, d_u, d_w)),
+        in_specs=specs,
+        out_specs=specs,
+        compiler_params=pltpu.CompilerParams(vmem_limit_bytes=60 * 1024 * 1024),
+    )(dg, d_a, d_u, d_w)
     d_a, d_u = (jnp.swapaxes(v, 0, 1)[None, None] for v in (d_a, d_u))
     return (dg.T, d_a, d_u, d_w)
 

time: 96.4 us -> 93.5 us (0.970)
  local copies, waits for them, and re-layouts: 7.28 us -> 0 us
  Pallas kernels: 88.2 us -> 92.7 us
    unnamed x6 -> x0, local copies, waits for them, and re-layouts: 7.28 us -> none
    pallas_call x0 -> x1, Pallas kernels: none -> 5.15 us  [local_kernel(): pl.pallas_call(place_kernel, grid=(steps,), out_shape=tuple((jax.ShapeDty...]
where the time goes in v4:
time: 93.5 us; the launch traced here: 93.3 us
  Pallas kernels  92.7 us (99%)
    pallas_call x1, Pallas kernels, local_kernel(): pl.pallas_call(whole_kernel, out_shape=(jax.ShapeDtypeStruct((4, 128), f4...  87.5 us
    pallas_call x1, Pallas kernels, local_kernel(): pl.pallas_call(place_kernel, grid=(steps,), out_shape=tuple((jax.ShapeDty...  5.15 us

profile of v4, /device:TPU:0, one launch (start us, length us, event | category | flops | bytes accessed | tf_op | source)
XLA Modules:
  0.0 93.3 jit_solution(16147212153300785374)
XLA Ops:
  0.6 87.5 %shard_map.93 = (f32[4,128]{1,0:T(4,128)}, bf16[68,8,768]{2,1,0:T(8,128)(2,1)}, bf16[68,8,768]{2,1,0:T(8,128)(2,1)}, bf16[1,2048,768]{2,1,0:T(8,128)(2,1)}) custom-call(s32[4,128]{1,0:T(4,128)} %bitcast.17, bf16[4,128]{1,0:T(4,128)(2,1)} %bitcast.18, bf16[128,4096]{1,0:T(8,128)(2,1)} %gout.1, bf16[68,8,768]{2,1,0:T(8,128)(2,1)} %bitcast.15, ...), custom_call_target="tpu_custom_call" | custom-call | tf_op jit(solution)/shard_map/pallas_call | solution.py:359
  88.2 5.1 %shard_map.94 = (f32[4,128]{1,0:T(4,128)}, bf16[68,8,768]{2,1,0:T(8,128)(2,1)}, bf16[68,8,768]{2,1,0:T(8,128)(2,1)}, bf16[1,2048,768]{2,1,0:T(8,128)(2,1)}) custom-call(f32[4,128]{1,0:T(4,128)} %get-tuple-element.12.dg, bf16[68,8,768]{2,1,0:T(8,128)(2,1)} %get-tuple-element.13.d_a, bf16[68,8,768]{2,1,0:T(8,128)(2,1)} %get-tuple-element.14.d_u, ...), custom_call_target="tpu_custom_call" | custom-call | tf_op jit(solution)/shard_map/pallas_call | solution.py:408
